TPU v7x, 32 devices: a whole 2x2x4 slice. The times are simulated.
32 devices in a mesh: row: 8 (over z, x), vec: 4 (over y, core).
Axes of the slice: x: 2, y: 2, z: 4, core: 2. Of those that a mesh axis runs over, the one named last changes fastest.
Arguments:
- vectors: bfloat16 [8192, 1024], P(('row', 'vec')), may hold values from -6 to 6
- rotation: bfloat16 [1024, 1024], replicated, may hold values from -0.1875 to 0.1875
- blocks: bfloat16 [64, 8, 128, 128], P('row'), may hold values from -0.1875 to 0.1875
- columns: int32 [64, 8], P('row'), may hold values from 0 to 63, as said below
Outputs:
- filtered: bfloat16 [8192, 1024], P('row', 'vec')
Inputs may be any that keep to these rules, and one draw needn't show every extreme that they name: `columns`: block row i stores its own block first, then block max(i - 6, 0), then block min(i + 2, 63); every other entry lies between i - 6 and i + 2, clipped to the grid.
All inputs are finite; a program needn't handle non-finite values.
Results may differ from a plain program's by a relative error of at most 0.0065.
Values may be sent and summed in bfloat16 or wider, within the bound.
A program may use at most 64 MiB of HBM per device.

v0:
```python
import jax
import jax.numpy as jnp
from jax import lax
from jax.sharding import PartitionSpec as P

DEG = 4
REACH_LO = 6
REACH_HI = 2


def extended_2(cells, sides, width):
    for axis, dim in sides:
        count = lax.axis_size(axis)
        ends = count - 1
        head = lax.slice_in_dim(cells, 0, width, axis=dim)
        tail = lax.slice_in_dim(cells, cells.shape[dim] - width, cells.shape[dim], axis=dim)
        cells = jnp.concatenate(
            [
                lax.ppermute(tail, axis, [(i, (i + 1) % count) for i in range(ends)]),
                cells,
                lax.ppermute(head, axis, [((i + 1) % count, i) for i in range(ends)]),
            ],
            axis=dim,
        )
    return cells


def per_device(vectors, rotation, blocks, columns):
    rotated = jnp.dot(vectors, rotation, preferred_element_type=jnp.float32).astype(jnp.bfloat16)
    panel = lax.all_to_all(rotated, "vec", split_axis=1, concat_axis=0, tiled=True)
    local_blocks = blocks.shape[0]
    block_rows = blocks.shape[2]
    group_width = panel.shape[1]
    first_block = lax.axis_index("row") * local_blocks

    def extend(state_bf):
        reach_blocks = max(REACH_LO, REACH_HI)
        wider = extended_2(state_bf, (("row", 0),), reach_blocks * block_rows)
        return (wider, reach_blocks)

    def apply_operator(state_bf):
        extended, offset = extend(state_bf)
        tiles = extended.reshape(-1, block_rows, group_width)
        local_index = columns - first_block + offset
        picked = tiles[local_index]
        result = jnp.einsum("bjrc,bjcv->brv", blocks, picked, preferred_element_type=jnp.float32)
        return result.reshape(local_blocks * block_rows, group_width)

    prev = panel.astype(jnp.float32)
    cur = (apply_operator(panel) - 0.25 * prev) / 2.0
    for degree in range(DEG - 1):
        sent = cur.astype(jnp.bfloat16)
        nxt = 2.0 * (apply_operator(sent) - 0.25 * cur) / 2.0 - prev
        prev = cur
        cur = nxt
    return cur.astype(jnp.bfloat16)


def solution(mesh):
    return jax.shard_map(
        per_device,
        mesh=mesh,
        in_specs=(P(("row", "vec"), None), P(), P("row", None, None, None), P("row", None)),
        out_specs=P("row", "vec"),
        check_vma=False,
    )
```

profile of v0, /device:TPU:25, one launch (start us, length us, event | category | flops | bytes accessed | tf_op | source)
XLA Modules:
  0.0 139.1 jit_solution(6693398314109884634)
XLA Ops:
  0.0 2.6 %convolution_convert_fusion = bf16[256,1024]{1,0:T(8,128)(2,1)S(1)} fusion(bf16[256,1024]{1,0:T(8,128)(2,1)} %param.4, bf16[1024,1024]{1,0:T(8,128)(2,1)} %param.5), kind=kOutput, calls=%fused_computation.10 | convolution fusion | flops 537133056 | bytes 3145728 | tf_op jit(solution)/shard_map/dot_general | solution.py:29
  2.7 11.1 %all_to_all.19 = bf16[256,4,256]{2,0,1:T(8,128)(2,1)S(1)} all-to-all(bf16[256,4,256]{2,0,1:T(8,128)(2,1)S(1)} %bitcast.112), channel_id=1, replica_groups=mesh['row'=8,'vec'=4] {'vec'}, dimensions={1} | all-to-all | bytes 1048576 | tf_op jit(solution)/shard_map/all_to_all | solution.py:30
  13.7 0.9 fusion.9
  14.7 3.0 %collective-permute-start.1 = (bf16[768,256]{1,0:T(8,128)(2,1)}, bf16[768,256]{1,0:T(8,128)(2,1)S(1)}, u32[]{:S(2)}, u32[]{:S(2)}) collective-permute-start(bf16[768,256]{1,0:T(8,128)(2,1)} %bitcast.3), channel_id=1, source_target_pairs={{4,0},{8,4},{12,8},{16,12},{20,16},{24,20},{28,24},{5,1},{9,5},{13... | collective-permute-start | bytes 1179656 | tf_op jit(solution)/shard_map/ppermute | solution.py:21
  17.7 2.3 %collective-permute-start = (bf16[768,256]{1,0:T(8,128)(2,1)}, bf16[768,256]{1,0:T(8,128)(2,1)S(1)}, u32[]{:S(2)}, u32[]{:S(2)}) collective-permute-start(bf16[768,256]{1,0:T(8,128)(2,1)} %bitcast.1), channel_id=1, source_target_pairs={{0,4},{4,8},{8,12},{12,16},{16,20},{20,24},{24,28},{1,5},{5,9},{9,... | collective-permute-start | bytes 1179656 | tf_op jit(solution)/shard_map/ppermute | solution.py:19
  20.1 14.7 %collective-permute-done.1 = bf16[768,256]{1,0:T(8,128)(2,1)S(1)} collective-permute-done((bf16[768,256]{1,0:T(8,128)(2,1)}, bf16[768,256]{1,0:T(8,128)(2,1)S(1)}, u32[]{:S(2)}, u32[]{:S(2)}) %collective-permute-start.1) | collective-permute-done | bytes 393248 | tf_op jit(solution)/shard_map/ppermute | solution.py:21
  34.8 1.2 pad_maximum_fusion
  35.9 4.1 %gather_fusion = bf16[64,128,256]{2,1,0:T(8,128)(2,1)} fusion(bf16[20,128,256]{2,1,0:T(8,128)(2,1)} %bitcast.107, s32[1024]{0:T(1024)S(1)} %pad_clamp_fusion), kind=kCustom, calls=%fused_computation | custom fusion | bytes 8388864 | tf_op jit(solution)/shard_map/gather | solution.py:45
  40.0 3.0 %fusion.10 = f32[8,256,128,1]{1,2,3,0:T(8,128)S(1)} fusion(bf16[8,8,128,128]{3,2,1,0:T(8,128)(2,1)S(1)} %copy-done, bf16[8,8,128,256]{3,2,1,0:T(8,128)(2,1)} %bitcast.109), kind=kOutput, calls=%fused_computation.28 | convolution fusion | flops 536870912 | bytes 7340032 | tf_op jit(solution)/shard_map/bjrc,bjcv->brv/dot_general | solution.py:46
  43.3 1.9 %collective-permute-start.2 = (bf16[768,256]{1,0:T(8,128)(2,1)S(1)}, bf16[768,256]{1,0:T(8,128)(2,1)S(1)}, u32[]{:S(2)}, u32[]{:S(2)}) collective-permute-start(bf16[768,256]{1,0:T(8,128)(2,1)S(1)} %get-tuple-element.9), channel_id=1, source_target_pairs={{0,4},{4,8},{8,12},{12,16},{16,20},{20,24},{24,28},{1,5},{5,9},{9,... | collective-permute-start | bytes 1179656 | tf_op jit(solution)/shard_map/ppermute | solution.py:19
  45.2 5.4 %collective-permute-start.3 = (bf16[768,256]{1,0:T(8,128)(2,1)S(1)}, bf16[768,256]{1,0:T(8,128)(2,1)S(1)}, u32[]{:S(2)}, u32[]{:S(2)}) collective-permute-start(bf16[768,256]{1,0:T(8,128)(2,1)S(1)} %get-tuple-element.10), channel_id=1, source_target_pairs={{4,0},{8,4},{12,8},{16,12},{20,16},{24,20},{28,24},{5,1},{9,5},{13... | collective-permute-start | bytes 1179656 | tf_op jit(solution)/shard_map/ppermute | solution.py:21
  50.6 6.5 %collective-permute-done.2 = bf16[768,256]{1,0:T(8,128)(2,1)S(1)} collective-permute-done((bf16[768,256]{1,0:T(8,128)(2,1)S(1)}, bf16[768,256]{1,0:T(8,128)(2,1)S(1)}, u32[]{:S(2)}, u32[]{:S(2)}) %collective-permute-start.2) | collective-permute-done | bytes 393248 | tf_op jit(solution)/shard_map/ppermute | solution.py:19
  57.1 9.4 %collective-permute-done.3 = bf16[768,256]{1,0:T(8,128)(2,1)S(1)} collective-permute-done((bf16[768,256]{1,0:T(8,128)(2,1)S(1)}, bf16[768,256]{1,0:T(8,128)(2,1)S(1)}, u32[]{:S(2)}, u32[]{:S(2)}) %collective-permute-start.3) | collective-permute-done | bytes 393248 | tf_op jit(solution)/shard_map/ppermute | solution.py:21
  66.5 1.2 pad_maximum_fusion.1
  67.7 4.1 %gather_fusion.1 = bf16[64,128,256]{2,1,0:T(8,128)(2,1)} fusion(bf16[20,128,256]{2,1,0:T(8,128)(2,1)} %bitcast.105, s32[1024]{0:T(1024)S(1)} %pad_clamp_fusion), kind=kCustom, calls=%fused_computation.1 | custom fusion | bytes 8388864 | tf_op jit(solution)/shard_map/gather | solution.py:45
  71.8 3.1 %fusion.11 = f32[8,256,128,1]{1,2,3,0:T(8,128)S(1)} fusion(bf16[8,8,128,128]{3,2,1,0:T(8,128)(2,1)S(1)} %copy-done, bf16[8,8,128,256]{3,2,1,0:T(8,128)(2,1)} %bitcast.110), kind=kOutput, calls=%fused_computation.29 | convolution fusion | flops 536870912 | bytes 7340032 | tf_op jit(solution)/shard_map/bjrc,bjcv->brv/dot_general | solution.py:46
  75.2 1.9 %collective-permute-start.4 = (bf16[768,256]{1,0:T(8,128)(2,1)S(1)}, bf16[768,256]{1,0:T(8,128)(2,1)S(1)}, u32[]{:S(2)}, u32[]{:S(2)}) collective-permute-start(bf16[768,256]{1,0:T(8,128)(2,1)S(1)} %get-tuple-element.7), channel_id=1, source_target_pairs={{0,4},{4,8},{8,12},{12,16},{16,20},{20,24},{24,28},{1,5},{5,9},{9,... | collective-permute-start | bytes 1179656 | tf_op jit(solution)/shard_map/ppermute | solution.py:19
  77.2 4.3 %collective-permute-start.5 = (bf16[768,256]{1,0:T(8,128)(2,1)S(1)}, bf16[768,256]{1,0:T(8,128)(2,1)S(1)}, u32[]{:S(2)}, u32[]{:S(2)}) collective-permute-start(bf16[768,256]{1,0:T(8,128)(2,1)S(1)} %get-tuple-element.8), channel_id=1, source_target_pairs={{4,0},{8,4},{12,8},{16,12},{20,16},{24,20},{28,24},{5,1},{9,5},{13... | collective-permute-start | bytes 1179656 | tf_op jit(solution)/shard_map/ppermute | solution.py:21
  81.4 6.7 %collective-permute-done.4 = bf16[768,256]{1,0:T(8,128)(2,1)S(1)} collective-permute-done((bf16[768,256]{1,0:T(8,128)(2,1)S(1)}, bf16[768,256]{1,0:T(8,128)(2,1)S(1)}, u32[]{:S(2)}, u32[]{:S(2)}) %collective-permute-start.4) | collective-permute-done | bytes 393248 | tf_op jit(solution)/shard_map/ppermute | solution.py:19
  88.2 9.3 %collective-permute-done.5 = bf16[768,256]{1,0:T(8,128)(2,1)S(1)} collective-permute-done((bf16[768,256]{1,0:T(8,128)(2,1)S(1)}, bf16[768,256]{1,0:T(8,128)(2,1)S(1)}, u32[]{:S(2)}, u32[]{:S(2)}) %collective-permute-start.5) | collective-permute-done | bytes 393248 | tf_op jit(solution)/shard_map/ppermute | solution.py:21
  97.5 1.2 pad_maximum_fusion.2
  98.7 4.1 %gather_fusion.2 = bf16[64,128,256]{2,1,0:T(8,128)(2,1)} fusion(bf16[20,128,256]{2,1,0:T(8,128)(2,1)} %bitcast.106, s32[1024]{0:T(1024)S(1)} %pad_clamp_fusion), kind=kCustom, calls=%fused_computation.2 | custom fusion | bytes 8388864 | tf_op jit(solution)/shard_map/gather | solution.py:45
  102.8 3.2 %fusion.12 = f32[8,256,128,1]{1,2,3,0:T(8,128)S(1)} fusion(bf16[8,8,128,128]{3,2,1,0:T(8,128)(2,1)S(1)} %copy-done, bf16[8,8,128,256]{3,2,1,0:T(8,128)(2,1)} %bitcast.111), kind=kOutput, calls=%fused_computation.30 | convolution fusion | flops 536870912 | bytes 7340032 | tf_op jit(solution)/shard_map/bjrc,bjcv->brv/dot_general | solution.py:46
  106.5 0.5 copy-done.8
  107.0 1.9 %collective-permute-start.6 = (bf16[768,256]{1,0:T(8,128)(2,1)S(1)}, bf16[768,256]{1,0:T(8,128)(2,1)S(1)}, u32[]{:S(2)}, u32[]{:S(2)}) collective-permute-start(bf16[768,256]{1,0:T(8,128)(2,1)S(1)} %get-tuple-element.5), channel_id=1, source_target_pairs={{0,4},{4,8},{8,12},{12,16},{16,20},{20,24},{24,28},{1,5},{5,9},{9,... | collective-permute-start | bytes 1179656 | tf_op jit(solution)/shard_map/ppermute | solution.py:19
  108.9 4.3 %collective-permute-start.7 = (bf16[768,256]{1,0:T(8,128)(2,1)S(1)}, bf16[768,256]{1,0:T(8,128)(2,1)S(1)}, u32[]{:S(2)}, u32[]{:S(2)}) collective-permute-start(bf16[768,256]{1,0:T(8,128)(2,1)S(1)} %get-tuple-element.6), channel_id=1, source_target_pairs={{4,0},{8,4},{12,8},{16,12},{20,16},{24,20},{28,24},{5,1},{9,5},{13... | collective-permute-start | bytes 1179656 | tf_op jit(solution)/shard_map/ppermute | solution.py:21
  113.2 6.8 %collective-permute-done.6 = bf16[768,256]{1,0:T(8,128)(2,1)S(1)} collective-permute-done((bf16[768,256]{1,0:T(8,128)(2,1)S(1)}, bf16[768,256]{1,0:T(8,128)(2,1)S(1)}, u32[]{:S(2)}, u32[]{:S(2)}) %collective-permute-start.6) | collective-permute-done | bytes 393248 | tf_op jit(solution)/shard_map/ppermute | solution.py:19
  120.0 9.2 %collective-permute-done.7 = bf16[768,256]{1,0:T(8,128)(2,1)S(1)} collective-permute-done((bf16[768,256]{1,0:T(8,128)(2,1)S(1)}, bf16[768,256]{1,0:T(8,128)(2,1)S(1)}, u32[]{:S(2)}, u32[]{:S(2)}) %collective-permute-start.7) | collective-permute-done | bytes 393248 | tf_op jit(solution)/shard_map/ppermute | solution.py:21
  129.3 1.2 pad_maximum_fusion.3
  130.4 4.1 %gather_fusion.3 = bf16[64,128,256]{2,1,0:T(8,128)(2,1)} fusion(bf16[20,128,256]{2,1,0:T(8,128)(2,1)} %bitcast.104, s32[1024]{0:T(1024)S(1)} %pad_clamp_fusion), kind=kCustom, calls=%fused_computation.3 | custom fusion | bytes 8388864 | tf_op jit(solution)/shard_map/gather | solution.py:45
  134.5 3.2 %fusion.13 = f32[8,256,128,1]{1,2,3,0:T(8,128)S(1)} fusion(bf16[8,8,128,128]{3,2,1,0:T(8,128)(2,1)S(1)} %copy-done, bf16[8,8,128,256]{3,2,1,0:T(8,128)(2,1)} %bitcast.108), kind=kOutput, calls=%fused_computation.31 | convolution fusion | flops 536870912 | bytes 7340032 | tf_op jit(solution)/shard_map/bjrc,bjcv->brv/dot_general | solution.py:46
  137.7 1.4 fusion.2
  (32 shorter events, 1.3 us)
Async XLA Ops:
  0.0 40.0 %copy-start = (bf16[8,8,128,128]{3,2,1,0:T(8,128)(2,1)S(1)}, bf16[8,8,128,128]{3,2,1,0:T(8,128)(2,1)}, u32[]{:S(2)}) copy-start(bf16[8,8,128,128]{3,2,1,0:T(8,128)(2,1)} %param.6) | copy-start | bytes 6291460
  2.6 17.4 %copy-start.10 = (s32[8,8]{1,0:T(8,128)S(1)}, s32[8,8]{1,0:T(8,128)}, u32[]{:S(2)}) copy-start(s32[8,8]{1,0:T(8,128)} %param.7) | copy-start | bytes 772
  14.7 20.1 %collective-permute-start.1 = (bf16[768,256]{1,0:T(8,128)(2,1)}, bf16[768,256]{1,0:T(8,128)(2,1)S(1)}, u32[]{:S(2)}, u32[]{:S(2)}) collective-permute-start(bf16[768,256]{1,0:T(8,128)(2,1)} %bitcast.3), channel_id=1, source_target_pairs={{4,0},{8,4},{12,8},{16,12},{20,16},{24,20},{28,24},{5,1},{9,5},{13... | collective-permute-start | bytes 1179656 | tf_op jit(solution)/shard_map/ppermute | solution.py:21
  17.7 17.1 %collective-permute-start = (bf16[768,256]{1,0:T(8,128)(2,1)}, bf16[768,256]{1,0:T(8,128)(2,1)S(1)}, u32[]{:S(2)}, u32[]{:S(2)}) collective-permute-start(bf16[768,256]{1,0:T(8,128)(2,1)} %bitcast.1), channel_id=1, source_target_pairs={{0,4},{4,8},{8,12},{12,16},{16,20},{20,24},{24,28},{1,5},{5,9},{9,... | collective-permute-start | bytes 1179656 | tf_op jit(solution)/shard_map/ppermute | solution.py:19
  43.0 24.7 %copy-start.1 = (f32[8,256,128,1]{1,2,3,0:T(8,128)}, f32[8,256,128,1]{1,2,3,0:T(8,128)S(1)}, u32[]{:S(2)}) copy-start(f32[8,256,128,1]{1,2,3,0:T(8,128)S(1)} %fusion.10) | copy-start | bytes 3145732
  43.3 13.8 %collective-permute-start.2 = (bf16[768,256]{1,0:T(8,128)(2,1)S(1)}, bf16[768,256]{1,0:T(8,128)(2,1)S(1)}, u32[]{:S(2)}, u32[]{:S(2)}) collective-permute-start(bf16[768,256]{1,0:T(8,128)(2,1)S(1)} %get-tuple-element.9), channel_id=1, source_target_pairs={{0,4},{4,8},{8,12},{12,16},{16,20},{20,24},{24,28},{1,5},{5,9},{9,... | collective-permute-start | bytes 1179656 | tf_op jit(solution)/shard_map/ppermute | solution.py:19
  45.2 21.3 %collective-permute-start.3 = (bf16[768,256]{1,0:T(8,128)(2,1)S(1)}, bf16[768,256]{1,0:T(8,128)(2,1)S(1)}, u32[]{:S(2)}, u32[]{:S(2)}) collective-permute-start(bf16[768,256]{1,0:T(8,128)(2,1)S(1)} %get-tuple-element.10), channel_id=1, source_target_pairs={{4,0},{8,4},{12,8},{16,12},{20,16},{24,20},{28,24},{5,1},{9,5},{13... | collective-permute-start | bytes 1179656 | tf_op jit(solution)/shard_map/ppermute | solution.py:21
  71.8 3.1 %copy-start.2 = (f32[8,256,128,1]{1,2,3,0:T(8,128)S(1)}, f32[8,256,128,1]{1,2,3,0:T(8,128)}, u32[]{:S(2)}) copy-start(f32[8,256,128,1]{1,2,3,0:T(8,128)} %copy-done.1) | copy-start | bytes 3145732
  74.9 23.8 %copy-start.5 = (f32[8,256,128,1]{1,2,3,0:T(8,128)}, f32[8,256,128,1]{1,2,3,0:T(8,128)S(1)}, u32[]{:S(2)}) copy-start(f32[8,256,128,1]{1,2,3,0:T(8,128)S(1)} %fusion.11) | copy-start | bytes 3145732
  75.2 12.9 %collective-permute-start.4 = (bf16[768,256]{1,0:T(8,128)(2,1)S(1)}, bf16[768,256]{1,0:T(8,128)(2,1)S(1)}, u32[]{:S(2)}, u32[]{:S(2)}) collective-permute-start(bf16[768,256]{1,0:T(8,128)(2,1)S(1)} %get-tuple-element.7), channel_id=1, source_target_pairs={{0,4},{4,8},{8,12},{12,16},{16,20},{20,24},{24,28},{1,5},{5,9},{9,... | collective-permute-start | bytes 1179656 | tf_op jit(solution)/shard_map/ppermute | solution.py:19
  77.2 20.3 %collective-permute-start.5 = (bf16[768,256]{1,0:T(8,128)(2,1)S(1)}, bf16[768,256]{1,0:T(8,128)(2,1)S(1)}, u32[]{:S(2)}, u32[]{:S(2)}) collective-permute-start(bf16[768,256]{1,0:T(8,128)(2,1)S(1)} %get-tuple-element.8), channel_id=1, source_target_pairs={{4,0},{8,4},{12,8},{16,12},{20,16},{24,20},{28,24},{5,1},{9,5},{13... | collective-permute-start | bytes 1179656 | tf_op jit(solution)/shard_map/ppermute | solution.py:21
  102.8 3.2 %copy-start.3 = (f32[8,256,128,1]{1,2,3,0:T(8,128)S(1)}, f32[8,256,128,1]{1,2,3,0:T(8,128)}, u32[]{:S(2)}) copy-start(f32[8,256,128,1]{1,2,3,0:T(8,128)} %copy-done.1) | copy-start | bytes 3145732
  102.8 3.2 %copy-start.6 = (f32[8,256,128,1]{1,2,3,0:T(8,128)S(1)}, f32[8,256,128,1]{1,2,3,0:T(8,128)}, u32[]{:S(2)}) copy-start(f32[8,256,128,1]{1,2,3,0:T(8,128)} %copy-done.5) | copy-start | bytes 3145732
  105.9 1.1 copy-start.8
  107.0 13.0 %collective-permute-start.6 = (bf16[768,256]{1,0:T(8,128)(2,1)S(1)}, bf16[768,256]{1,0:T(8,128)(2,1)S(1)}, u32[]{:S(2)}, u32[]{:S(2)}) collective-permute-start(bf16[768,256]{1,0:T(8,128)(2,1)S(1)} %get-tuple-element.5), channel_id=1, source_target_pairs={{0,4},{4,8},{8,12},{12,16},{16,20},{20,24},{24,28},{1,5},{5,9},{9,... | collective-permute-start | bytes 1179656 | tf_op jit(solution)/shard_map/ppermute | solution.py:19
  108.9 20.3 %collective-permute-start.7 = (bf16[768,256]{1,0:T(8,128)(2,1)S(1)}, bf16[768,256]{1,0:T(8,128)(2,1)S(1)}, u32[]{:S(2)}, u32[]{:S(2)}) collective-permute-start(bf16[768,256]{1,0:T(8,128)(2,1)S(1)} %get-tuple-element.6), channel_id=1, source_target_pairs={{4,0},{8,4},{12,8},{16,12},{20,16},{24,20},{28,24},{5,1},{9,5},{13... | collective-permute-start | bytes 1179656 | tf_op jit(solution)/shard_map/ppermute | solution.py:21
  134.5 3.2 %copy-start.4 = (f32[8,256,128,1]{1,2,3,0:T(8,128)S(1)}, f32[8,256,128,1]{1,2,3,0:T(8,128)}, u32[]{:S(2)}) copy-start(f32[8,256,128,1]{1,2,3,0:T(8,128)} %copy-done.1) | copy-start | bytes 3145732
  134.5 3.2 %copy-start.7 = (f32[8,256,128,1]{1,2,3,0:T(8,128)S(1)}, f32[8,256,128,1]{1,2,3,0:T(8,128)}, u32[]{:S(2)}) copy-start(f32[8,256,128,1]{1,2,3,0:T(8,128)} %copy-done.5) | copy-start | bytes 3145732
  134.5 3.2 %copy-start.9 = (f32[8,256,128,1]{1,2,3,0:T(8,128)S(1)}, f32[8,256,128,1]{1,2,3,0:T(8,128)}, u32[]{:S(2)}) copy-start(f32[8,256,128,1]{1,2,3,0:T(8,128)} %copy-done.8) | copy-start | bytes 3145732
where the time goes:
time: 140 us; the launch traced here: 139 us
  waiting for transfers between devices  62.7 us (45%)
  starting transfers between devices  24.9 us (18%)
  local copies, waits for them, and re-layouts  18.1 us (13%)
  matrix products  15 us (11%)
  blocking collectives  11.1 us (8%)
  other arithmetic  7.06 us (5%)
    ppermute x4, waiting for transfers between devices, extended_2(): lax.ppermute(head, axis, [((i + 1) % count, i) for i in range(ends)])  42.6 us
    ppermute x4, waiting for transfers between devices, extended_2(): lax.ppermute(tail, axis, [(i, (i + 1) % count) for i in range(ends)])  20 us
    ppermute x4, starting transfers between devices, extended_2(): lax.ppermute(head, axis, [((i + 1) % count, i) for i in range(ends)])  16.9 us
    gather x4, local copies, waits for them, and re-layouts, apply_operator(): picked = tiles[local_index]  16.3 us
    dot_general x4, matrix products, apply_operator(): jnp.einsum('bjrc,bjcv->brv', blocks, picked, preferred_element_type=jnp.f...  12.4 us
    all_to_all x1, blocking collectives, per_device(): lax.all_to_all(rotated, 'vec', split_axis=1, concat_axis=0, tiled=True)  11.1 us
    ppermute x4, starting transfers between devices, extended_2(): lax.ppermute(tail, axis, [(i, (i + 1) % count) for i in range(ends)])  8.05 us
    concatenate x4, other arithmetic, extended_2(): jnp.concatenate([lax.ppermute(tail, axis, [(i, (i + 1) % count) for i in...  4.73 us
  transfers between devices with their start and end apart: 8, of which 7 were waited for; matrix products, arithmetic and copies ran while one was open for 0% of the time, Pallas kernels for 0%

commit v1 on v0

v1 whole, which is shorter than its diff:
```python
import functools

import jax
import jax.numpy as jnp
from jax import lax
from jax.experimental import pallas as pl
from jax.experimental.pallas import tpu as pltpu
from jax.sharding import PartitionSpec as P

DEG = 4
REACH_LO = 6
REACH_HI = 2
LANES = 128
MESH = pl.DeviceIdType.MESH


def filter_kernel(
    rows, groups, halves, chunks,
    vec_hbm, rot_hbm, blk_hbm, cols_in, out_hbm,
    *scratch,
):
    refs = list(scratch)
    take = lambda n: [refs.pop(0) for _ in range(n)]
    ext = [take(halves) for _ in range(DEG)]
    state = [take(halves) for _ in range(2)]
    res = take(halves)
    vec_v, rot_v, sendbuf, blk_v, cols_v, cols_s = take(6)
    (load_sem, cols_send, cols_recv, a2a_send, a2a_recv, blk_send, blk_recv,
     fwd_send, fwd_recv, halo_send, halo_recv, out_send, out_recv) = take(13)

    local, nnz, bs, _ = blk_v.shape
    span = ext[0][0].shape[0]
    tiles, width = sendbuf.shape[2], sendbuf.shape[4]
    half_rows = local // 2
    step = half_rows // chunks

    r, v = lax.axis_index("row"), lax.axis_index("vec")
    z, x = r // 2, r % 2
    y, c = v // 2, v % 2
    s, g = 2 * z + c, 2 * y + x
    home = x == c
    away = x != c
    first = s * local

    def device_of(sup, grp):
        return (2 * (sup // 2) + grp % 2, 2 * (grp // 2) + sup % 2)

    partner = (2 * z + 1 - x, 2 * y + 1 - c)
    across = (r, 2 * (y + 1 - 2 * (y % 2)) + c)
    has_low, has_up = s > 0, s < rows - 1
    low, up = device_of(s - 1, g), device_of(s + 1, g)
    far_low = jnp.logical_and(has_low, c == 0)
    far_up = jnp.logical_and(has_up, c == 1)

    barrier = pltpu.get_barrier_semaphore()
    for k in range(1, 2 * groups):
        q = (x * groups + v + k) % (2 * groups)
        pl.semaphore_signal(
            barrier, inc=1, device_id=(2 * z + q // groups, q % groups), device_id_type=MESH)

    @pl.when(far_low)
    def _():
        pl.semaphore_signal(barrier, inc=1, device_id=low, device_id_type=MESH)

    @pl.when(far_up)
    def _():
        pl.semaphore_signal(barrier, inc=1, device_id=up, device_id_type=MESH)

    vec_copy = pltpu.make_async_copy(vec_hbm, vec_v, load_sem.at[0])
    vec_copy.start()
    rot_copies = []
    for k in range(groups):
        cols = pl.ds(pl.multiple_of(((g + 1 + k) % groups) * (halves * width), LANES), halves * width)
        rot_copies.append(
            pltpu.make_async_copy(rot_hbm.at[:, cols], rot_v.at[:, cols], load_sem.at[3 + k]))
        rot_copies[-1].start()
    blk_copy = pltpu.make_async_copy(blk_hbm, blk_v, load_sem.at[1])

    @pl.when(home)
    def _():
        blk_copy.start()

    layers = jnp.where(jnp.logical_or(far_low, far_up), 1, 0)
    pl.semaphore_wait(barrier, 2 * groups - 1 + layers)

    cols_copy = pltpu.make_async_remote_copy(
        src_ref=cols_in, dst_ref=cols_v, send_sem=cols_send, recv_sem=cols_recv,
        device_id=partner, device_id_type=MESH)

    def direct(k):
        part = pl.ds((y % 2) * half_rows + k * step, step)
        return pltpu.make_async_remote_copy(
            src_ref=blk_hbm.at[part], dst_ref=blk_v.at[part],
            send_sem=blk_send.at[k], recv_sem=blk_recv.at[k],
            device_id=partner, device_id_type=MESH)

    def forward(k, mine=True):
        side = y % 2 if mine else 1 - y % 2
        part = pl.ds(side * half_rows + k * step, step)
        return pltpu.make_async_remote_copy(
            src_ref=blk_v.at[part], dst_ref=blk_v.at[part],
            send_sem=fwd_send.at[k], recv_sem=fwd_recv.at[k],
            device_id=across, device_id_type=MESH)

    @pl.when(away)
    def _():
        cols_copy.start()
        direct(0).start()

    def a2a(grp, h):
        return pltpu.make_async_remote_copy(
            src_ref=sendbuf.at[grp, h],
            dst_ref=ext[0][h].at[pl.ds(REACH_LO + v * tiles, tiles)],
            send_sem=a2a_send.at[grp, h], recv_sem=a2a_recv.at[v, h],
            device_id=device_of(r, grp), device_id_type=MESH)

    vec_copy.wait()
    for k in range(groups):
        rot_copies[k].wait()
        grp = (g + 1 + k) % groups
        cols = pl.ds(pl.multiple_of(grp * (halves * width), LANES), halves * width)
        piece = jnp.dot(vec_v[...], rot_v[:, cols], preferred_element_type=jnp.float32)
        piece = piece.astype(jnp.bfloat16)
        own = jnp.logical_and(home, grp == g)
        for h in range(halves):
            part = piece[:, h * width:(h + 1) * width].reshape(tiles, bs, width)

            @pl.when(own)
            def _():
                ext[0][h][pl.ds(REACH_LO + v * tiles, tiles)] = part

            @pl.when(jnp.logical_not(own))
            def _():
                sendbuf[grp, h] = part
                a2a(grp, h).start()

    @pl.when(away)
    def _():
        for k in range(1, chunks):
            direct(k).start()

    def up_copy(d, h):
        return pltpu.make_async_remote_copy(
            src_ref=ext[d][h].at[pl.ds(local, REACH_LO)],
            dst_ref=ext[d][h].at[pl.ds(0, REACH_LO)],
            send_sem=halo_send.at[d, h, 0], recv_sem=halo_recv.at[d, h, 0],
            device_id=up, device_id_type=MESH)

    def down_copy(d, h):
        return pltpu.make_async_remote_copy(
            src_ref=ext[d][h].at[pl.ds(REACH_LO, REACH_HI)],
            dst_ref=ext[d][h].at[pl.ds(REACH_LO + local, REACH_HI)],
            send_sem=halo_send.at[d, h, 1], recv_sem=halo_recv.at[d, h, 1],
            device_id=low, device_id_type=MESH)

    def start_up(d, h):
        @pl.when(has_up)
        def _():
            up_copy(d, h).start()

    def start_down(d, h):
        @pl.when(has_low)
        def _():
            down_copy(d, h).start()

    def wait_halo(d, h):
        @pl.when(has_low)
        def _():
            up_copy(d, h).wait_recv()

        @pl.when(has_up)
        def _():
            down_copy(d, h).wait_recv()

    for h in range(halves):
        for src in range(groups):
            @pl.when(jnp.logical_not(jnp.logical_and(home, v == src)))
            def _():
                pltpu.make_async_remote_copy(
                    src_ref=sendbuf.at[0, h],
                    dst_ref=ext[0][h].at[pl.ds(REACH_LO + src * tiles, tiles)],
                    send_sem=a2a_send.at[0, h], recv_sem=a2a_recv.at[src, h],
                    device_id=partner, device_id_type=MESH).wait_recv()
        start_up(0, h)
        start_down(0, h)

    @pl.when(away)
    def _():
        cols_copy.wait()
        to_smem = pltpu.make_async_copy(cols_v, cols_s, load_sem.at[2])
        to_smem.start()
        to_smem.wait()
        for k in range(chunks):
            direct(k).wait_recv()
            forward(k).start()
        for k in range(chunks):
            forward(k, mine=False).wait_recv()

    @pl.when(home)
    def _():
        to_smem = pltpu.make_async_copy(cols_in, cols_s, load_sem.at[2])
        to_smem.start()
        to_smem.wait()
        blk_copy.wait()

    def apply_rows(d, h, lo, hi):
        def one_row(i, carry):
            lhs = jnp.concatenate([blk_v[i, j] for j in range(nnz)], axis=1)
            rhs = jnp.concatenate(
                [ext[d][h][jnp.clip(cols_s[i, j] - first + REACH_LO, 0, span - 1)] for j in range(nnz)],
                axis=0)
            acc = jnp.dot(lhs, rhs, preferred_element_type=jnp.float32)
            if d == 0:
                old = ext[0][h][REACH_LO + i].astype(jnp.float32)
                new = (acc - 0.25 * old) / 2.0
            else:
                cur = state[(d - 1) % 2][h][i]
                if d == 1:
                    prev = ext[0][h][REACH_LO + i].astype(jnp.float32)
                else:
                    prev = state[d % 2][h][i]
                new = (acc - 0.25 * cur) - prev
            if d < DEG - 1:
                state[d % 2][h][i] = new
                ext[d + 1][h][REACH_LO + i] = new.astype(jnp.bfloat16)
            else:
                res[h][i] = new.astype(jnp.bfloat16)
            return carry

        lax.fori_loop(lo, hi, one_row, 0, unroll=True)

    def out_part(h):
        return out_hbm.at[:, :, pl.ds(h * width, width)]

    def out_remote(h):
        return pltpu.make_async_remote_copy(
            src_ref=res[h], dst_ref=out_part(h),
            send_sem=out_send.at[h], recv_sem=out_recv.at[h],
            device_id=partner, device_id_type=MESH)

    def out_local(h):
        return pltpu.make_async_copy(res[h], out_part(h), out_send.at[h])

    for d in range(DEG):
        for h in range(halves):
            wait_halo(d, h)
            if d < DEG - 1:
                apply_rows(d, h, local - REACH_LO, local)
                start_up(d + 1, h)
                apply_rows(d, h, 0, local - REACH_LO)
                start_down(d + 1, h)
            else:
                apply_rows(d, h, 0, local)

                @pl.when(away)
                def _():
                    out_remote(h).start()

                @pl.when(home)
                def _():
                    out_local(h).start()

    for k in range(groups):
        grp = (g + 1 + k) % groups
        for h in range(halves):
            @pl.when(jnp.logical_not(jnp.logical_and(home, grp == g)))
            def _():
                a2a(grp, h).wait_send()
    for d in range(DEG):
        for h in range(halves):
            @pl.when(has_up)
            def _():
                up_copy(d, h).wait_send()

            @pl.when(has_low)
            def _():
                down_copy(d, h).wait_send()

    @pl.when(away)
    def _():
        for k in range(chunks):
            direct(k).wait_send()
            forward(k).wait_send()
        for h in range(halves):
            out_remote(h).wait()

    @pl.when(home)
    def _():
        for h in range(halves):
            out_local(h).wait()


def solution(mesh):
    rows, groups = mesh.shape["row"], mesh.shape["vec"]

    def per_device(vectors, rotation, blocks, columns):
        height, nv = vectors.shape
        local, nnz, bs, _ = blocks.shape
        group_width = nv // groups
        width = min(group_width, LANES)
        halves = group_width // width
        chunks = 4 if local % 8 == 0 else 1
        tiles = height // bs
        bf16, f32 = jnp.bfloat16, jnp.float32
        dma = pltpu.SemaphoreType.DMA
        span = REACH_LO + local + REACH_HI
        flops = 2 * height * nv * nv + 2 * DEG * local * nnz * bs * bs * group_width
        out = pl.pallas_call(
            functools.partial(filter_kernel, rows, groups, halves, chunks),
            out_shape=jax.ShapeDtypeStruct((local, bs, group_width), bf16),
            in_specs=[
                pl.BlockSpec(memory_space=pl.ANY),
                pl.BlockSpec(memory_space=pl.ANY),
                pl.BlockSpec(memory_space=pl.ANY),
                pl.BlockSpec(memory_space=pltpu.VMEM),
            ],
            out_specs=pl.BlockSpec(memory_space=pl.ANY),
            scratch_shapes=(
                [pltpu.VMEM((span, bs, width), bf16)] * (DEG * halves)
                + [pltpu.VMEM((local, bs, width), f32)] * (2 * halves)
                + [pltpu.VMEM((local, bs, width), bf16)] * halves
                + [
                    pltpu.VMEM((height, nv), bf16),
                    pltpu.VMEM((nv, nv), bf16),
                    pltpu.VMEM((groups, halves, tiles, bs, width), bf16),
                    pltpu.VMEM((local, nnz, bs, bs), bf16),
                    pltpu.VMEM(columns.shape, jnp.int32),
                    pltpu.SMEM(columns.shape, jnp.int32),
                    dma((3 + groups,)),
                    dma, dma,
                    dma((groups, halves)), dma((groups, halves)),
                    dma((chunks,)), dma((chunks,)),
                    dma((chunks,)), dma((chunks,)),
                    dma((DEG, halves, 2)), dma((DEG, halves, 2)),
                    dma((halves,)), dma((halves,)),
                ]
            ),
            compiler_params=pltpu.CompilerParams(
                collective_id=0, has_side_effects=True, vmem_limit_bytes=40 * 2**20),
            cost_estimate=pl.CostEstimate(
                flops=flops, bytes_accessed=8 * 2**20, transcendentals=0),
        )(vectors, rotation, blocks, columns)
        return out.reshape(local * bs, group_width)

    return jax.shard_map(
        per_device,
        mesh=mesh,
        in_specs=(P(("row", "vec"), None), P(), P("row", None, None, None), P("row", None)),
        out_specs=P("row", "vec"),
        check_vma=False,
    )
```

time: 140 us -> 56.1 us (0.40)
  waiting for transfers between devices: 62.7 us -> 0 us
  Pallas kernels: 0 us -> 50.1 us
  starting transfers between devices: 24.9 us -> 0 us
  matrix products: 15 us -> 0 us
  local copies, waits for them, and re-layouts: 18.1 us -> 5.7 us
  blocking collectives: 11.1 us -> 0 us
  other arithmetic: 7.06 us -> 0 us
    ppermute x8 -> x0, waiting for transfers between devices: 62.7 us -> none  [the longest x4 42.6 us: extended_2(): lax.ppermute(head, axis, [((i + 1) % count, i) for i in range(ends)])]
    pallas_call x0 -> x1, Pallas kernels: none -> 50.1 us  [per_device(): pl.pallas_call(functools.partial(filter_kernel, rows, groups, halves, chu...]
    ppermute x8 -> x0, starting transfers between devices: 24.9 us -> none  [the longest x4 16.9 us: extended_2(): lax.ppermute(head, axis, [((i + 1) % count, i) for i in range(ends)])]
    gather x4 -> x0, local copies, waits for them, and re-layouts: 16.3 us -> none  [apply_operator(): picked = tiles[local_index]]
    dot_general x5 -> x0, matrix products: 15 us -> none  [the longest x4 12.4 us: apply_operator(): jnp.einsum('bjrc,bjcv->brv', blocks, picked, preferred_element_type=jnp.f...]
    all_to_all x1 -> x0, blocking collectives: 11.1 us -> none  [per_device(): lax.all_to_all(rotated, 'vec', split_axis=1, concat_axis=0, tiled=True)]
    unnamed x22 -> x9, local copies, waits for them, and re-layouts: 0.58 us -> 5.7 us
    concatenate x4 -> x0, other arithmetic: 4.73 us -> none  [extended_2(): jnp.concatenate([lax.ppermute(tail, axis, [(i, (i + 1) % count) for i in...]
  transfers between devices with their start and end apart: 8 -> 0, of which waited for: 7 -> 0; matrix products, arithmetic and copies ran while one was open for 0% -> 0% of each run, Pallas kernels for 0% -> 0%
where the time goes in v1:
time: 56.1 us; the launch traced here: 55.8 us
  Pallas kernels  50.1 us (89%)
  local copies, waits for them, and re-layouts  5.7 us (10%)
    pallas_call x1, Pallas kernels, per_device(): pl.pallas_call(functools.partial(filter_kernel, rows, groups, halves, chu...  50.1 us
    unnamed x9, local copies, waits for them, and re-layouts  5.7 us

profile of v1, /device:TPU:25, one launch (start us, length us, event | category | flops | bytes accessed | tf_op | source)
XLA Modules:
  0.0 55.8 jit_solution(6530372154337671377)
XLA Ops:
  0.0 0.0 copy-start
  0.0 1.6 %copy-done = bf16[1024,1024]{1,0:T(8,128)(2,1)S(1)} copy-done((bf16[1024,1024]{1,0:T(8,128)(2,1)S(1)}, bf16[1024,1024]{1,0:T(8,128)(2,1)}, u32[]{:S(2)}) %copy-start) | copy-done | bytes 2097176
  1.6 0.0 copy-start.1
  1.6 1.6 %copy-done.1 = bf16[8,8,128,128]{3,2,1,0:T(8,128)(2,1)S(1)} copy-done((bf16[8,8,128,128]{3,2,1,0:T(8,128)(2,1)S(1)}, bf16[8,8,128,128]{3,2,1,0:T(8,128)(2,1)}, u32[]{:S(2)}) %copy-start.1) | copy-done | bytes 2097176
  3.2 0.0 copy-start.2
  3.2 1.0 %copy-done.2 = bf16[256,1024]{1,0:T(8,128)(2,1)S(1)} copy-done((bf16[256,1024]{1,0:T(8,128)(2,1)S(1)}, bf16[256,1024]{1,0:T(8,128)(2,1)}, u32[]{:S(2)}) %copy-start.2) | copy-done | bytes 524312
  4.2 0.0 copy-start.3
  4.2 0.7 %copy-done.3 = s32[8,8]{1,0:T(8,128)S(1)} copy-done((s32[8,8]{1,0:T(8,128)S(1)}, s32[8,8]{1,0:T(8,128)}, u32[]{:S(2)}) %copy-start.3) | copy-done | bytes 280
  4.9 50.1 %shard_map.46 = bf16[8,128,256]{2,1,0:T(8,128)(2,1)S(1)} custom-call(bf16[256,1024]{1,0:T(8,128)(2,1)S(1)} %copy-done.2, bf16[1024,1024]{1,0:T(8,128)(2,1)S(1)} %copy-done, bf16[8,8,128,128]{3,2,1,0:T(8,128)(2,1)S(1)} %copy-done.1, s32[8,8]{1,0:T(8,128)S(1)} %copy-done.3), custom_call_target="tpu_custom_call" | custom-call | flops 2684354560 | bytes 8388608 | tf_op jit(solution)/shard_map/pallas_call | solution.py:308
  55.0 0.8 %copy.6 = bf16[1024,256]{1,0:T(8,128)(2,1)} copy(bf16[1024,256]{1,0:T(8,128)(2,1)S(1)} %bitcast.1) | data formatting | bytes 1048576
Async XLA Ops:
  0.0 1.6 %copy-start = (bf16[1024,1024]{1,0:T(8,128)(2,1)S(1)}, bf16[1024,1024]{1,0:T(8,128)(2,1)}, u32[]{:S(2)}) copy-start(bf16[1024,1024]{1,0:T(8,128)(2,1)} %rot_hbm.1) | copy-start | bytes 6291460
  1.6 1.6 %copy-start.1 = (bf16[8,8,128,128]{3,2,1,0:T(8,128)(2,1)S(1)}, bf16[8,8,128,128]{3,2,1,0:T(8,128)(2,1)}, u32[]{:S(2)}) copy-start(bf16[8,8,128,128]{3,2,1,0:T(8,128)(2,1)} %blk_hbm.1) | copy-start | bytes 6291460
  3.2 1.0 %copy-start.2 = (bf16[256,1024]{1,0:T(8,128)(2,1)S(1)}, bf16[256,1024]{1,0:T(8,128)(2,1)}, u32[]{:S(2)}) copy-start(bf16[256,1024]{1,0:T(8,128)(2,1)} %vec_hbm.1) | copy-start | bytes 1572868
  4.2 0.7 %copy-start.3 = (s32[8,8]{1,0:T(8,128)S(1)}, s32[8,8]{1,0:T(8,128)}, u32[]{:S(2)}) copy-start(s32[8,8]{1,0:T(8,128)} %cols_in.1) | copy-start | bytes 772

commit v2 on v1

--- a/solution.py
+++ b/solution.py
@@ -15,7 +15,7 @@
 
 
 def filter_kernel(
-    rows, groups, halves, chunks,
+    rows, groups, halves, pieces,
     vec_hbm, rot_hbm, blk_hbm, cols_in, out_hbm,
     *scratch,
 ):
@@ -31,8 +31,7 @@
     local, nnz, bs, _ = blk_v.shape
     span = ext[0][0].shape[0]
     tiles, width = sendbuf.shape[2], sendbuf.shape[4]
-    half_rows = local // 2
-    step = half_rows // chunks
+    chunks = local
 
     r, v = lax.axis_index("row"), lax.axis_index("vec")
     z, x = r // 2, r % 2
@@ -87,25 +86,41 @@
         src_ref=cols_in, dst_ref=cols_v, send_sem=cols_send, recv_sem=cols_recv,
         device_id=partner, device_id_type=MESH)
 
-    def direct(k):
-        part = pl.ds((y % 2) * half_rows + k * step, step)
+    def chunk(q, side):
+        return (pl.ds(local - 1 - 2 * (q // 2) - side, 1), pl.ds((q % 2) * (nnz // 2), nnz // 2))
+
+    def direct(q):
+        part = chunk(q, y % 2)
         return pltpu.make_async_remote_copy(
             src_ref=blk_hbm.at[part], dst_ref=blk_v.at[part],
-            send_sem=blk_send.at[k], recv_sem=blk_recv.at[k],
+            send_sem=blk_send.at[q], recv_sem=blk_recv.at[q],
             device_id=partner, device_id_type=MESH)
 
-    def forward(k, mine=True):
-        side = y % 2 if mine else 1 - y % 2
-        part = pl.ds(side * half_rows + k * step, step)
+    def forward(q, mine=True):
+        part = chunk(q, y % 2 if mine else 1 - y % 2)
         return pltpu.make_async_remote_copy(
             src_ref=blk_v.at[part], dst_ref=blk_v.at[part],
-            send_sem=fwd_send.at[k], recv_sem=fwd_recv.at[k],
+            send_sem=fwd_send.at[q], recv_sem=fwd_recv.at[q],
             device_id=across, device_id_type=MESH)
 
+    def start_direct(lo, hi):
+        @pl.when(away)
+        def _():
+            for q in range(lo, hi):
+                direct(q).start()
+
+    def pass_on(lo, hi):
+        @pl.when(away)
+        def _():
+            for q in range(lo, hi):
+                direct(q).wait_recv()
+                forward(q).start()
+
     @pl.when(away)
     def _():
         cols_copy.start()
-        direct(0).start()
+
+    start_direct(0, 2)
 
     def a2a(grp, h):
         return pltpu.make_async_remote_copy(
@@ -134,10 +149,8 @@
                 sendbuf[grp, h] = part
                 a2a(grp, h).start()
 
-    @pl.when(away)
-    def _():
-        for k in range(1, chunks):
-            direct(k).start()
+    start_direct(2, 4)
+    pass_on(0, 2)
 
     def up_copy(d, h):
         return pltpu.make_async_remote_copy(
@@ -183,6 +196,10 @@
                     device_id=partner, device_id_type=MESH).wait_recv()
         start_up(0, h)
         start_down(0, h)
+        if h == 0:
+            start_direct(4, 6)
+    start_direct(6, chunks)
+    pass_on(2, 6)
 
     @pl.when(away)
     def _():
@@ -190,11 +207,6 @@
         to_smem = pltpu.make_async_copy(cols_v, cols_s, load_sem.at[2])
         to_smem.start()
         to_smem.wait()
-        for k in range(chunks):
-            direct(k).wait_recv()
-            forward(k).start()
-        for k in range(chunks):
-            forward(k, mine=False).wait_recv()
 
     @pl.when(home)
     def _():
@@ -203,45 +215,70 @@
         to_smem.wait()
         blk_copy.wait()
 
+    def one_row(d, h, i):
+        lhs = jnp.concatenate([blk_v[i, j] for j in range(nnz)], axis=1)
+        rhs = jnp.concatenate(
+            [ext[d][h][jnp.clip(cols_s[i, j] - first + REACH_LO, 0, span - 1)] for j in range(nnz)],
+            axis=0)
+        acc = jnp.dot(lhs, rhs, preferred_element_type=jnp.float32)
+        if d == 0:
+            old = ext[0][h][REACH_LO + i].astype(jnp.float32)
+            new = (acc - 0.25 * old) / 2.0
+        else:
+            cur = state[(d - 1) % 2][h][i]
+            if d == 1:
+                prev = ext[0][h][REACH_LO + i].astype(jnp.float32)
+            else:
+                prev = state[d % 2][h][i]
+            new = (acc - 0.25 * cur) - prev
+        if d < DEG - 1:
+            state[d % 2][h][i] = new
+            ext[d + 1][h][REACH_LO + i] = new.astype(jnp.bfloat16)
+        else:
+            res[h][i] = new.astype(jnp.bfloat16)
+
     def apply_rows(d, h, lo, hi):
-        def one_row(i, carry):
-            lhs = jnp.concatenate([blk_v[i, j] for j in range(nnz)], axis=1)
-            rhs = jnp.concatenate(
-                [ext[d][h][jnp.clip(cols_s[i, j] - first + REACH_LO, 0, span - 1)] for j in range(nnz)],
-                axis=0)
-            acc = jnp.dot(lhs, rhs, preferred_element_type=jnp.float32)
-            if d == 0:
-                old = ext[0][h][REACH_LO + i].astype(jnp.float32)
-                new = (acc - 0.25 * old) / 2.0
-            else:
-                cur = state[(d - 1) % 2][h][i]
-                if d == 1:
-                    prev = ext[0][h][REACH_LO + i].astype(jnp.float32)
-                else:
-                    prev = state[d % 2][h][i]
-                new = (acc - 0.25 * cur) - prev
-            if d < DEG - 1:
-                state[d % 2][h][i] = new
-                ext[d + 1][h][REACH_LO + i] = new.astype(jnp.bfloat16)
-            else:
-                res[h][i] = new.astype(jnp.bfloat16)
+        def body(i, carry):
+            one_row(d, h, i)
             return carry
 
-        lax.fori_loop(lo, hi, one_row, 0, unroll=True)
-
-    def out_part(h):
-        return out_hbm.at[:, :, pl.ds(h * width, width)]
-
-    def out_remote(h):
-        return pltpu.make_async_remote_copy(
-            src_ref=res[h], dst_ref=out_part(h),
-            send_sem=out_send.at[h], recv_sem=out_recv.at[h],
+        lax.fori_loop(lo, hi, body, 0, unroll=True)
+
+    def out_part(h, k):
+        part = pl.ds(k * (local // pieces), local // pieces)
+        return res[h].at[part], out_hbm.at[part, :, pl.ds(h * width, width)]
+
+    def out_remote(h, k):
+        src, dst = out_part(h, k)
+        return pltpu.make_async_remote_copy(
+            src_ref=src, dst_ref=dst, send_sem=out_send.at[h, k], recv_sem=out_recv.at[h, k],
             device_id=partner, device_id_type=MESH)
 
-    def out_local(h):
-        return pltpu.make_async_copy(res[h], out_part(h), out_send.at[h])
-
-    for d in range(DEG):
+    def out_local(h, k):
+        src, dst = out_part(h, k)
+        return pltpu.make_async_copy(src, dst, out_send.at[h, k])
+
+    for h in range(halves):
+        wait_halo(0, h)
+    for k in range(local // 2):
+        if 2 * k + 2 == chunks - 2:
+            pass_on(6, chunks)
+        for other in (False, True):
+            if other:
+                @pl.when(away)
+                def _():
+                    for q in (2 * k, 2 * k + 1):
+                        forward(q, mine=False).wait_recv()
+            row = local - 1 - 2 * k - (1 - y % 2 if other else y % 2)
+            for h in range(halves):
+                one_row(0, h, row)
+        if 2 * k + 2 == REACH_LO:
+            for h in range(halves):
+                start_up(1, h)
+    for h in range(halves):
+        start_down(1, h)
+
+    for d in range(1, DEG):
         for h in range(halves):
             wait_halo(d, h)
             if d < DEG - 1:
@@ -250,15 +287,16 @@
                 apply_rows(d, h, 0, local - REACH_LO)
                 start_down(d + 1, h)
             else:
-                apply_rows(d, h, 0, local)
-
-                @pl.when(away)
-                def _():
-                    out_remote(h).start()
-
-                @pl.when(home)
-                def _():
-                    out_local(h).start()
+                for k in range(pieces):
+                    apply_rows(d, h, k * (local // pieces), (k + 1) * (local // pieces))
+
+                    @pl.when(away)
+                    def _():
+                        out_remote(h, k).start()
+
+                    @pl.when(home)
+                    def _():
+                        out_local(h, k).start()
 
     for k in range(groups):
         grp = (g + 1 + k) % groups
@@ -282,12 +320,14 @@
             direct(k).wait_send()
             forward(k).wait_send()
         for h in range(halves):
-            out_remote(h).wait()
+            for k in range(pieces):
+                out_remote(h, k).wait()
 
     @pl.when(home)
     def _():
         for h in range(halves):
-            out_local(h).wait()
+            for k in range(pieces):
+                out_local(h, k).wait()
 
 
 def solution(mesh):
@@ -299,22 +339,22 @@
         group_width = nv // groups
         width = min(group_width, LANES)
         halves = group_width // width
-        chunks = 4 if local % 8 == 0 else 1
+        pieces, chunks = 2, local
         tiles = height // bs
         bf16, f32 = jnp.bfloat16, jnp.float32
         dma = pltpu.SemaphoreType.DMA
         span = REACH_LO + local + REACH_HI
         flops = 2 * height * nv * nv + 2 * DEG * local * nnz * bs * bs * group_width
         out = pl.pallas_call(
-            functools.partial(filter_kernel, rows, groups, halves, chunks),
+            functools.partial(filter_kernel, rows, groups, halves, pieces),
             out_shape=jax.ShapeDtypeStruct((local, bs, group_width), bf16),
             in_specs=[
-                pl.BlockSpec(memory_space=pl.ANY),
-                pl.BlockSpec(memory_space=pl.ANY),
-                pl.BlockSpec(memory_space=pl.ANY),
+                pl.BlockSpec(memory_space=pltpu.HBM),
+                pl.BlockSpec(memory_space=pltpu.HBM),
+                pl.BlockSpec(memory_space=pltpu.HBM),
                 pl.BlockSpec(memory_space=pltpu.VMEM),
             ],
-            out_specs=pl.BlockSpec(memory_space=pl.ANY),
+            out_specs=pl.BlockSpec(memory_space=pltpu.HBM),
             scratch_shapes=(
                 [pltpu.VMEM((span, bs, width), bf16)] * (DEG * halves)
                 + [pltpu.VMEM((local, bs, width), f32)] * (2 * halves)
@@ -332,7 +372,7 @@
                     dma((chunks,)), dma((chunks,)),
                     dma((chunks,)), dma((chunks,)),
                     dma((DEG, halves, 2)), dma((DEG, halves, 2)),
-                    dma((halves,)), dma((halves,)),
+                    dma((halves, pieces)), dma((halves, pieces)),
                 ]
             ),
             compiler_params=pltpu.CompilerParams(

time: 56.1 us -> 53 us (0.945)
  Pallas kernels: 50.1 us -> 47 us
    pallas_call x1, Pallas kernels: 50.1 us -> 47 us  [per_device(): pl.pallas_call(functools.partial(filter_kernel, rows, groups, halves, pie...]
where the time goes in v2:
time: 53 us; the launch traced here: 52.7 us
  Pallas kernels  47 us (89%)
  local copies, waits for them, and re-layouts  5.7 us (11%)
    pallas_call x1, Pallas kernels, per_device(): pl.pallas_call(functools.partial(filter_kernel, rows, groups, halves, pie...  47 us
    unnamed x9, local copies, waits for them, and re-layouts  5.7 us

profile of v2, /device:TPU:25, one launch (start us, length us, event | category | flops | bytes accessed | tf_op | source)
XLA Modules:
  0.0 52.7 jit_solution(8269033683410881323)
XLA Ops:
  0.0 0.0 copy-start
  0.0 1.6 %copy-done = bf16[1024,1024]{1,0:T(8,128)(2,1)S(1)} copy-done((bf16[1024,1024]{1,0:T(8,128)(2,1)S(1)}, bf16[1024,1024]{1,0:T(8,128)(2,1)}, u32[]{:S(2)}) %copy-start) | copy-done | bytes 2097176
  1.6 0.0 copy-start.1
  1.6 1.6 %copy-done.1 = bf16[8,8,128,128]{3,2,1,0:T(8,128)(2,1)S(1)} copy-done((bf16[8,8,128,128]{3,2,1,0:T(8,128)(2,1)S(1)}, bf16[8,8,128,128]{3,2,1,0:T(8,128)(2,1)}, u32[]{:S(2)}) %copy-start.1) | copy-done | bytes 2097176
  3.2 0.0 copy-start.2
  3.2 1.0 %copy-done.2 = bf16[256,1024]{1,0:T(8,128)(2,1)S(1)} copy-done((bf16[256,1024]{1,0:T(8,128)(2,1)S(1)}, bf16[256,1024]{1,0:T(8,128)(2,1)}, u32[]{:S(2)}) %copy-start.2) | copy-done | bytes 524312
  4.2 0.0 copy-start.3
  4.2 0.7 %copy-done.3 = s32[8,8]{1,0:T(8,128)S(1)} copy-done((s32[8,8]{1,0:T(8,128)S(1)}, s32[8,8]{1,0:T(8,128)}, u32[]{:S(2)}) %copy-start.3) | copy-done | bytes 280
  4.9 47.0 %shard_map.46 = bf16[8,128,256]{2,1,0:T(8,128)(2,1)S(1)} custom-call(bf16[256,1024]{1,0:T(8,128)(2,1)S(1)} %copy-done.2, bf16[1024,1024]{1,0:T(8,128)(2,1)S(1)} %copy-done, bf16[8,8,128,128]{3,2,1,0:T(8,128)(2,1)S(1)} %copy-done.1, s32[8,8]{1,0:T(8,128)S(1)} %copy-done.3), custom_call_target="tpu_custom_call" | custom-call | flops 2684354560 | bytes 8388608 | tf_op jit(solution)/shard_map/pallas_call | solution.py:348
  51.9 0.8 %copy.6 = bf16[1024,256]{1,0:T(8,128)(2,1)} copy(bf16[1024,256]{1,0:T(8,128)(2,1)S(1)} %bitcast.1) | data formatting | bytes 1048576
Async XLA Ops:
  0.0 1.6 %copy-start = (bf16[1024,1024]{1,0:T(8,128)(2,1)S(1)}, bf16[1024,1024]{1,0:T(8,128)(2,1)}, u32[]{:S(2)}) copy-start(bf16[1024,1024]{1,0:T(8,128)(2,1)} %rot_hbm.1) | copy-start | bytes 6291460
  1.6 1.6 %copy-start.1 = (bf16[8,8,128,128]{3,2,1,0:T(8,128)(2,1)S(1)}, bf16[8,8,128,128]{3,2,1,0:T(8,128)(2,1)}, u32[]{:S(2)}) copy-start(bf16[8,8,128,128]{3,2,1,0:T(8,128)(2,1)} %blk_hbm.1) | copy-start | bytes 6291460
  3.2 1.0 %copy-start.2 = (bf16[256,1024]{1,0:T(8,128)(2,1)S(1)}, bf16[256,1024]{1,0:T(8,128)(2,1)}, u32[]{:S(2)}) copy-start(bf16[256,1024]{1,0:T(8,128)(2,1)} %vec_hbm.1) | copy-start | bytes 1572868
  4.2 0.7 %copy-start.3 = (s32[8,8]{1,0:T(8,128)S(1)}, s32[8,8]{1,0:T(8,128)}, u32[]{:S(2)}) copy-start(s32[8,8]{1,0:T(8,128)} %cols_in.1) | copy-start | bytes 772

commit v3 on v2

--- a/solution.py
+++ b/solution.py
@@ -349,12 +349,12 @@
             functools.partial(filter_kernel, rows, groups, halves, pieces),
             out_shape=jax.ShapeDtypeStruct((local, bs, group_width), bf16),
             in_specs=[
-                pl.BlockSpec(memory_space=pltpu.HBM),
-                pl.BlockSpec(memory_space=pltpu.HBM),
-                pl.BlockSpec(memory_space=pltpu.HBM),
-                pl.BlockSpec(memory_space=pltpu.VMEM),
+                pl.BlockSpec(memory_space=pl.ANY),
+                pl.BlockSpec(memory_space=pl.ANY),
+                pl.BlockSpec(memory_space=pl.ANY),
+                pl.BlockSpec(memory_space=pl.ANY),
             ],
-            out_specs=pl.BlockSpec(memory_space=pltpu.HBM),
+            out_specs=pl.BlockSpec(memory_space=pl.ANY),
             scratch_shapes=(
                 [pltpu.VMEM((span, bs, width), bf16)] * (DEG * halves)
                 + [pltpu.VMEM((local, bs, width), f32)] * (2 * halves)
@@ -376,7 +376,7 @@
                 ]
             ),
             compiler_params=pltpu.CompilerParams(
-                collective_id=0, has_side_effects=True, vmem_limit_bytes=40 * 2**20),
+                collective_id=0, has_side_effects=True, vmem_limit_bytes=127 * 2**19),
             cost_estimate=pl.CostEstimate(
                 flops=flops, bytes_accessed=8 * 2**20, transcendentals=0),
         )(vectors, rotation, blocks, columns)

time: 53 us -> 49.3 us (0.930)
  local copies, waits for them, and re-layouts: 5.7 us -> 1.87 us
    unnamed x9 -> x1, local copies, waits for them, and re-layouts: 5.7 us -> 1.87 us
where the time goes in v3:
time: 49.3 us; the launch traced here: 49.2 us
  Pallas kernels  47.3 us (96%)
  local copies, waits for them, and re-layouts  1.87 us (4%)
    pallas_call x1, Pallas kernels, per_device(): pl.pallas_call(functools.partial(filter_kernel, rows, groups, halves, pie...  47.3 us
    unnamed x1, local copies, waits for them, and re-layouts  1.87 us

profile of v3, /device:TPU:25, one launch (start us, length us, event | category | flops | bytes accessed | tf_op | source)
XLA Modules:
  0.0 49.2 jit_solution(11147433941035725484)
XLA Ops:
  0.0 47.3 %shard_map.46 = bf16[8,128,256]{2,1,0:T(8,128)(2,1)} custom-call(bf16[256,1024]{1,0:T(8,128)(2,1)} %vec_hbm.1, bf16[1024,1024]{1,0:T(8,128)(2,1)} %rot_hbm.1, bf16[8,8,128,128]{3,2,1,0:T(8,128)(2,1)} %blk_hbm.1, s32[8,8]{1,0:T(8,128)} %cols_in.1), custom_call_target="tpu_custom_call" | custom-call | flops 2684354560 | bytes 8388608 | tf_op jit(solution)/shard_map/pallas_call | solution.py:348
  47.3 1.9 %copy.6 = bf16[1024,256]{1,0:T(8,128)(2,1)} copy(bf16[1024,256]{1,0:T(8,128)(2,1)} %bitcast.1) | data formatting | bytes 1048576

commit v4 on v3

--- a/solution.py
+++ b/solution.py
@@ -215,22 +215,29 @@
         to_smem.wait()
         blk_copy.wait()
 
+    def product(d, parts, i):
+        lhs = jnp.concatenate([blk_v[i, j] for j in range(nnz)], axis=1)
+        tile = [jnp.clip(cols_s[i, j] - first + REACH_LO, 0, span - 1) for j in range(nnz)]
+        rhs = [jnp.concatenate([ext[d][h][t] for t in tile], axis=0) for h in parts]
+        rhs = rhs[0] if len(parts) == 1 else jnp.concatenate(rhs, axis=1)
+        return jnp.dot(lhs, rhs, preferred_element_type=jnp.float32)
+
+    def first_row(i):
+        acc = product(0, range(halves), i)
+        for h in range(halves):
+            old = ext[0][h][REACH_LO + i].astype(jnp.float32)
+            new = (acc[:, h * width:(h + 1) * width] - 0.25 * old) / 2.0
+            state[0][h][i] = new
+            ext[1][h][REACH_LO + i] = new.astype(jnp.bfloat16)
+
     def one_row(d, h, i):
-        lhs = jnp.concatenate([blk_v[i, j] for j in range(nnz)], axis=1)
-        rhs = jnp.concatenate(
-            [ext[d][h][jnp.clip(cols_s[i, j] - first + REACH_LO, 0, span - 1)] for j in range(nnz)],
-            axis=0)
-        acc = jnp.dot(lhs, rhs, preferred_element_type=jnp.float32)
-        if d == 0:
-            old = ext[0][h][REACH_LO + i].astype(jnp.float32)
-            new = (acc - 0.25 * old) / 2.0
+        acc = product(d, (h,), i)
+        cur = state[(d - 1) % 2][h][i]
+        if d == 1:
+            prev = ext[0][h][REACH_LO + i].astype(jnp.float32)
         else:
-            cur = state[(d - 1) % 2][h][i]
-            if d == 1:
-                prev = ext[0][h][REACH_LO + i].astype(jnp.float32)
-            else:
-                prev = state[d % 2][h][i]
-            new = (acc - 0.25 * cur) - prev
+            prev = state[d % 2][h][i]
+        new = (acc - 0.25 * cur) - prev
         if d < DEG - 1:
             state[d % 2][h][i] = new
             ext[d + 1][h][REACH_LO + i] = new.astype(jnp.bfloat16)
@@ -246,7 +253,7 @@
 
     def out_part(h, k):
         part = pl.ds(k * (local // pieces), local // pieces)
-        return res[h].at[part], out_hbm.at[part, :, pl.ds(h * width, width)]
+        return res[h].at[part], out_hbm.at[h, part]
 
     def out_remote(h, k):
         src, dst = out_part(h, k)
@@ -270,8 +277,7 @@
                     for q in (2 * k, 2 * k + 1):
                         forward(q, mine=False).wait_recv()
             row = local - 1 - 2 * k - (1 - y % 2 if other else y % 2)
-            for h in range(halves):
-                one_row(0, h, row)
+            first_row(row)
         if 2 * k + 2 == REACH_LO:
             for h in range(halves):
                 start_up(1, h)
@@ -330,6 +336,12 @@
                 out_local(h, k).wait()
 
 
+def side_by_side(parts, whole):
+    halves, rows, bs, width = parts.shape
+    for h in range(halves):
+        whole[:, h * width:(h + 1) * width] = parts[h].reshape(rows * bs, width)
+
+
 def solution(mesh):
     rows, groups = mesh.shape["row"], mesh.shape["vec"]
 
@@ -339,7 +351,7 @@
         group_width = nv // groups
         width = min(group_width, LANES)
         halves = group_width // width
-        pieces, chunks = 2, local
+        pieces = 2
         tiles = height // bs
         bf16, f32 = jnp.bfloat16, jnp.float32
         dma = pltpu.SemaphoreType.DMA
@@ -347,7 +359,7 @@
         flops = 2 * height * nv * nv + 2 * DEG * local * nnz * bs * bs * group_width
         out = pl.pallas_call(
             functools.partial(filter_kernel, rows, groups, halves, pieces),
-            out_shape=jax.ShapeDtypeStruct((local, bs, group_width), bf16),
+            out_shape=jax.ShapeDtypeStruct((halves, local, bs, width), bf16),
             in_specs=[
                 pl.BlockSpec(memory_space=pl.ANY),
                 pl.BlockSpec(memory_space=pl.ANY),
@@ -369,8 +381,8 @@
                     dma((3 + groups,)),
                     dma, dma,
                     dma((groups, halves)), dma((groups, halves)),
-                    dma((chunks,)), dma((chunks,)),
-                    dma((chunks,)), dma((chunks,)),
+                    dma((local,)), dma((local,)),
+                    dma((local,)), dma((local,)),
                     dma((DEG, halves, 2)), dma((DEG, halves, 2)),
                     dma((halves, pieces)), dma((halves, pieces)),
                 ]
@@ -380,7 +392,14 @@
             cost_estimate=pl.CostEstimate(
                 flops=flops, bytes_accessed=8 * 2**20, transcendentals=0),
         )(vectors, rotation, blocks, columns)
-        return out.reshape(local * bs, group_width)
+        return pl.pallas_call(
+            side_by_side,
+            grid=(2,),
+            out_shape=jax.ShapeDtypeStruct((local * bs, group_width), bf16),
+            in_specs=[pl.BlockSpec((halves, local // 2, bs, width), lambda i: (0, i, 0, 0))],
+            out_specs=pl.BlockSpec((local // 2 * bs, group_width), lambda i: (i, 0)),
+            compiler_params=pltpu.CompilerParams(vmem_limit_bytes=8 * 2**20),
+        )(out)
 
     return jax.shard_map(
         per_device,

time: 49.3 us -> 49.4 us (level)
  local copies, waits for them, and re-layouts: 1.87 us -> 1.03 us
  Pallas kernels: 47.3 us -> 48.1 us
    pallas_call x0 -> x1, Pallas kernels: none -> 0.89 us  [per_device(): pl.pallas_call(side_by_side, grid=(2,), out_shape=jax.ShapeDtypeStruct((l...]
    unnamed x1 -> x2, local copies, waits for them, and re-layouts: 1.87 us -> 1.03 us
where the time goes in v4:
time: 49.4 us; the launch traced here: 49.2 us
  Pallas kernels  48.1 us (97%)
  local copies, waits for them, and re-layouts  1.03 us (2%)
    pallas_call x1, Pallas kernels, per_device(): pl.pallas_call(functools.partial(filter_kernel, rows, groups, halves, pie...  47.3 us
    unnamed x2, local copies, waits for them, and re-layouts  1.03 us

profile of v4, /device:TPU:25, one launch (start us, length us, event | category | flops | bytes accessed | tf_op | source)
XLA Modules:
  0.0 49.2 jit_solution(15409779965199921514)
XLA Ops:
  0.0 47.3 %shard_map.46.parts = bf16[2,8,128,128]{3,2,1,0:T(8,128)(2,1)} custom-call(bf16[256,1024]{1,0:T(8,128)(2,1)} %vec_hbm.1, bf16[1024,1024]{1,0:T(8,128)(2,1)} %rot_hbm.1, bf16[8,8,128,128]{3,2,1,0:T(8,128)(2,1)} %blk_hbm.1, s32[8,8]{1,0:T(8,128)} %cols_in.1), custom_call_target="tpu_custom_call" | custom-call | flops 2684354560 | bytes 8388608 | tf_op jit(solution)/shard_map/pallas_call | solution.py:360
  47.3 0.0 copy-start
  47.3 1.0 %copy-done = bf16[2,8,128,128]{3,2,1,0:T(8,128)(2,1)S(1)} copy-done((bf16[2,8,128,128]{3,2,1,0:T(8,128)(2,1)S(1)}, bf16[2,8,128,128]{3,2,1,0:T(8,128)(2,1)}, u32[]{:S(2)}) %copy-start) | copy-done | bytes 524312
  48.3 0.9 %shard_map.47 = bf16[1024,256]{1,0:T(8,128)(2,1)} custom-call(bf16[2,8,128,128]{3,2,1,0:T(8,128)(2,1)S(1)} %copy-done), custom_call_target="tpu_custom_call" | custom-call | tf_op jit(solution)/shard_map/pallas_call | solution.py:395
Async XLA Ops:
  47.3 1.0 %copy-start = (bf16[2,8,128,128]{3,2,1,0:T(8,128)(2,1)S(1)}, bf16[2,8,128,128]{3,2,1,0:T(8,128)(2,1)}, u32[]{:S(2)}) copy-start(bf16[2,8,128,128]{3,2,1,0:T(8,128)(2,1)} %shard_map.46.parts) | copy-start | bytes 1572868

commit v5 on v4

--- a/solution.py
+++ b/solution.py
@@ -120,7 +120,7 @@
     def _():
         cols_copy.start()
 
-    start_direct(0, 2)
+    start_direct(0, 3)
 
     def a2a(grp, h):
         return pltpu.make_async_remote_copy(
@@ -132,6 +132,8 @@
     vec_copy.wait()
     for k in range(groups):
         rot_copies[k].wait()
+        if k == groups - 1:
+            pass_on(0, 1)
         grp = (g + 1 + k) % groups
         cols = pl.ds(pl.multiple_of(grp * (halves * width), LANES), halves * width)
         piece = jnp.dot(vec_v[...], rot_v[:, cols], preferred_element_type=jnp.float32)
@@ -149,8 +151,8 @@
                 sendbuf[grp, h] = part
                 a2a(grp, h).start()
 
-    start_direct(2, 4)
-    pass_on(0, 2)
+    start_direct(3, 5)
+    pass_on(1, 2)
 
     def up_copy(d, h):
         return pltpu.make_async_remote_copy(
@@ -197,9 +199,9 @@
         start_up(0, h)
         start_down(0, h)
         if h == 0:
-            start_direct(4, 6)
+            start_direct(5, 6)
     start_direct(6, chunks)
-    pass_on(2, 6)
+    pass_on(2, chunks - 2)
 
     @pl.when(away)
     def _():
@@ -268,8 +270,8 @@
     for h in range(halves):
         wait_halo(0, h)
     for k in range(local // 2):
-        if 2 * k + 2 == chunks - 2:
-            pass_on(6, chunks)
+        if k in (1, 2):
+            pass_on(chunks - 3 + k, chunks - 2 + k)
         for other in (False, True):
             if other:
                 @pl.when(away)

time: 49.4 us -> 49.8 us (level)
  Pallas kernels: 48.1 us -> 48.6 us
where the time goes in v5:
time: 49.8 us; the launch traced here: 49.6 us
  Pallas kernels  48.6 us (98%)
  local copies, waits for them, and re-layouts  1.03 us (2%)
    pallas_call x1, Pallas kernels, per_device(): pl.pallas_call(functools.partial(filter_kernel, rows, groups, halves, pie...  47.7 us
    unnamed x2, local copies, waits for them, and re-layouts  1.03 us

profile of v5, /device:TPU:25, one launch (start us, length us, event | category | flops | bytes accessed | tf_op | source)
XLA Modules:
  0.0 49.6 jit_solution(3947236204383323834)
XLA Ops:
  0.0 47.7 %shard_map.46.parts = bf16[2,8,128,128]{3,2,1,0:T(8,128)(2,1)} custom-call(bf16[256,1024]{1,0:T(8,128)(2,1)} %vec_hbm.1, bf16[1024,1024]{1,0:T(8,128)(2,1)} %rot_hbm.1, bf16[8,8,128,128]{3,2,1,0:T(8,128)(2,1)} %blk_hbm.1, s32[8,8]{1,0:T(8,128)} %cols_in.1), custom_call_target="tpu_custom_call" | custom-call | flops 2684354560 | bytes 8388608 | tf_op jit(solution)/shard_map/pallas_call | solution.py:362
  47.7 0.0 copy-start
  47.7 1.0 %copy-done = bf16[2,8,128,128]{3,2,1,0:T(8,128)(2,1)S(1)} copy-done((bf16[2,8,128,128]{3,2,1,0:T(8,128)(2,1)S(1)}, bf16[2,8,128,128]{3,2,1,0:T(8,128)(2,1)}, u32[]{:S(2)}) %copy-start) | copy-done | bytes 524312
  48.7 0.9 %shard_map.47 = bf16[1024,256]{1,0:T(8,128)(2,1)} custom-call(bf16[2,8,128,128]{3,2,1,0:T(8,128)(2,1)S(1)} %copy-done), custom_call_target="tpu_custom_call" | custom-call | tf_op jit(solution)/shard_map/pallas_call | solution.py:397
Async XLA Ops:
  47.7 1.0 %copy-start = (bf16[2,8,128,128]{3,2,1,0:T(8,128)(2,1)S(1)}, bf16[2,8,128,128]{3,2,1,0:T(8,128)(2,1)}, u32[]{:S(2)}) copy-start(bf16[2,8,128,128]{3,2,1,0:T(8,128)(2,1)} %shard_map.46.parts) | copy-start | bytes 1572868

commit v6 on v4

--- a/solution.py
+++ b/solution.py
@@ -15,7 +15,7 @@
 
 
 def filter_kernel(
-    rows, groups, halves, pieces,
+    rows, groups, halves,
     vec_hbm, rot_hbm, blk_hbm, cols_in, out_hbm,
     *scratch,
 ):
@@ -86,18 +86,24 @@
         src_ref=cols_in, dst_ref=cols_v, send_sem=cols_send, recv_sem=cols_recv,
         device_id=partner, device_id_type=MESH)
 
-    def chunk(q, side):
-        return (pl.ds(local - 1 - 2 * (q // 2) - side, 1), pl.ds((q % 2) * (nnz // 2), nnz // 2))
+    pairs = local // 2
+
+    def pair_at(k, parity):
+        return k + parity * (pairs - 1 - 2 * k)
+
+    def chunk(q, side, parity):
+        row = 2 * pair_at(q // 2, parity) + side
+        return (pl.ds(row, 1), pl.ds((q % 2) * (nnz // 2), nnz // 2))
 
     def direct(q):
-        part = chunk(q, y % 2)
+        part = chunk(q, y % 2, 1 - c)
         return pltpu.make_async_remote_copy(
             src_ref=blk_hbm.at[part], dst_ref=blk_v.at[part],
             send_sem=blk_send.at[q], recv_sem=blk_recv.at[q],
             device_id=partner, device_id_type=MESH)
 
     def forward(q, mine=True):
-        part = chunk(q, y % 2 if mine else 1 - y % 2)
+        part = chunk(q, y % 2 if mine else 1 - y % 2, c)
         return pltpu.make_async_remote_copy(
             src_ref=blk_v.at[part], dst_ref=blk_v.at[part],
             send_sem=fwd_send.at[q], recv_sem=fwd_recv.at[q],
@@ -152,34 +158,46 @@
     start_direct(2, 4)
     pass_on(0, 2)
 
-    def up_copy(d, h):
-        return pltpu.make_async_remote_copy(
-            src_ref=ext[d][h].at[pl.ds(local, REACH_LO)],
-            dst_ref=ext[d][h].at[pl.ds(0, REACH_LO)],
-            send_sem=halo_send.at[d, h, 0], recv_sem=halo_recv.at[d, h, 0],
+    ups = REACH_LO // 2
+
+    def up_copy(d, h, p):
+        return pltpu.make_async_remote_copy(
+            src_ref=ext[d][h].at[pl.ds(local + 2 * p, 2)],
+            dst_ref=ext[d][h].at[pl.ds(2 * p, 2)],
+            send_sem=halo_send.at[d, h, p], recv_sem=halo_recv.at[d, h, p],
             device_id=up, device_id_type=MESH)
 
     def down_copy(d, h):
         return pltpu.make_async_remote_copy(
             src_ref=ext[d][h].at[pl.ds(REACH_LO, REACH_HI)],
             dst_ref=ext[d][h].at[pl.ds(REACH_LO + local, REACH_HI)],
-            send_sem=halo_send.at[d, h, 1], recv_sem=halo_recv.at[d, h, 1],
+            send_sem=halo_send.at[d, h, ups], recv_sem=halo_recv.at[d, h, ups],
             device_id=low, device_id_type=MESH)
 
-    def start_up(d, h):
-        @pl.when(has_up)
-        def _():
-            up_copy(d, h).start()
-
-    def start_down(d, h):
-        @pl.when(has_low)
-        def _():
-            down_copy(d, h).start()
+    def send_pair(d, h, pair):
+        if pair * 2 < REACH_HI:
+            @pl.when(has_low)
+            def _():
+                down_copy(d, h).start()
+        if pair >= pairs - ups:
+            @pl.when(has_up)
+            def _():
+                up_copy(d, h, pair - (pairs - ups)).start()
+
+    def send_after(d, h, k):
+        @pl.when(c == 0)
+        def _():
+            send_pair(d, h, k)
+
+        @pl.when(c == 1)
+        def _():
+            send_pair(d, h, pairs - 1 - k)
 
     def wait_halo(d, h):
         @pl.when(has_low)
         def _():
-            up_copy(d, h).wait_recv()
+            for p in range(ups):
+                up_copy(d, h, p).wait_recv()
 
         @pl.when(has_up)
         def _():
@@ -194,8 +212,8 @@
                     dst_ref=ext[0][h].at[pl.ds(REACH_LO + src * tiles, tiles)],
                     send_sem=a2a_send.at[0, h], recv_sem=a2a_recv.at[src, h],
                     device_id=partner, device_id_type=MESH).wait_recv()
-        start_up(0, h)
-        start_down(0, h)
+        for k in range(pairs):
+            send_after(0, h, k)
         if h == 0:
             start_direct(4, 6)
     start_direct(6, chunks)
@@ -244,16 +262,9 @@
         else:
             res[h][i] = new.astype(jnp.bfloat16)
 
-    def apply_rows(d, h, lo, hi):
-        def body(i, carry):
-            one_row(d, h, i)
-            return carry
-
-        lax.fori_loop(lo, hi, body, 0, unroll=True)
-
-    def out_part(h, k):
-        part = pl.ds(k * (local // pieces), local // pieces)
-        return res[h].at[part], out_hbm.at[h, part]
+    def out_part(h, k, parity=c):
+        part = pl.ds(2 * pair_at(k, parity), 2)
+        return res[h].at[part], out_hbm.at[part, :, pl.ds(h * width, width)]
 
     def out_remote(h, k):
         src, dst = out_part(h, k)
@@ -267,35 +278,28 @@
 
     for h in range(halves):
         wait_halo(0, h)
-    for k in range(local // 2):
-        if 2 * k + 2 == chunks - 2:
-            pass_on(6, chunks)
-        for other in (False, True):
-            if other:
+    for k in range(pairs):
+        if k == pairs - 2:
+            pass_on(chunks - 2, chunks)
+        for side in range(2):
+            if side == 1:
                 @pl.when(away)
                 def _():
                     for q in (2 * k, 2 * k + 1):
                         forward(q, mine=False).wait_recv()
-            row = local - 1 - 2 * k - (1 - y % 2 if other else y % 2)
-            first_row(row)
-        if 2 * k + 2 == REACH_LO:
-            for h in range(halves):
-                start_up(1, h)
-    for h in range(halves):
-        start_down(1, h)
+            first_row(2 * pair_at(k, c) + (1 - y % 2 if side else y % 2))
+        for h in range(halves):
+            send_after(1, h, k)
 
     for d in range(1, DEG):
         for h in range(halves):
             wait_halo(d, h)
-            if d < DEG - 1:
-                apply_rows(d, h, local - REACH_LO, local)
-                start_up(d + 1, h)
-                apply_rows(d, h, 0, local - REACH_LO)
-                start_down(d + 1, h)
-            else:
-                for k in range(pieces):
-                    apply_rows(d, h, k * (local // pieces), (k + 1) * (local // pieces))
-
+            for k in range(pairs):
+                for side in range(2):
+                    one_row(d, h, 2 * pair_at(k, c) + side)
+                if d < DEG - 1:
+                    send_after(d + 1, h, k)
+                else:
                     @pl.when(away)
                     def _():
                         out_remote(h, k).start()
@@ -314,7 +318,8 @@
         for h in range(halves):
             @pl.when(has_up)
             def _():
-                up_copy(d, h).wait_send()
+                for p in range(ups):
+                    up_copy(d, h, p).wait_send()
 
             @pl.when(has_low)
             def _():
@@ -326,20 +331,14 @@
             direct(k).wait_send()
             forward(k).wait_send()
         for h in range(halves):
-            for k in range(pieces):
+            for k in range(pairs):
                 out_remote(h, k).wait()
 
     @pl.when(home)
     def _():
         for h in range(halves):
-            for k in range(pieces):
+            for k in range(pairs):
                 out_local(h, k).wait()
-
-
-def side_by_side(parts, whole):
-    halves, rows, bs, width = parts.shape
-    for h in range(halves):
-        whole[:, h * width:(h + 1) * width] = parts[h].reshape(rows * bs, width)
 
 
 def solution(mesh):
@@ -351,15 +350,14 @@
         group_width = nv // groups
         width = min(group_width, LANES)
         halves = group_width // width
-        pieces = 2
         tiles = height // bs
         bf16, f32 = jnp.bfloat16, jnp.float32
         dma = pltpu.SemaphoreType.DMA
         span = REACH_LO + local + REACH_HI
         flops = 2 * height * nv * nv + 2 * DEG * local * nnz * bs * bs * group_width
         out = pl.pallas_call(
-            functools.partial(filter_kernel, rows, groups, halves, pieces),
-            out_shape=jax.ShapeDtypeStruct((halves, local, bs, width), bf16),
+            functools.partial(filter_kernel, rows, groups, halves),
+            out_shape=jax.ShapeDtypeStruct((local, bs, group_width), bf16),
             in_specs=[
                 pl.BlockSpec(memory_space=pl.ANY),
                 pl.BlockSpec(memory_space=pl.ANY),
@@ -383,23 +381,16 @@
                     dma((groups, halves)), dma((groups, halves)),
                     dma((local,)), dma((local,)),
                     dma((local,)), dma((local,)),
-                    dma((DEG, halves, 2)), dma((DEG, halves, 2)),
-                    dma((halves, pieces)), dma((halves, pieces)),
+                    dma((DEG, halves, REACH_LO // 2 + 1)), dma((DEG, halves, REACH_LO // 2 + 1)),
+                    dma((halves, local // 2)), dma((halves, local // 2)),
                 ]
             ),
             compiler_params=pltpu.CompilerParams(
-                collective_id=0, has_side_effects=True, vmem_limit_bytes=127 * 2**19),
+                collective_id=0, has_side_effects=True, vmem_limit_bytes=253 * 2**18),
             cost_estimate=pl.CostEstimate(
                 flops=flops, bytes_accessed=8 * 2**20, transcendentals=0),
         )(vectors, rotation, blocks, columns)
-        return pl.pallas_call(
-            side_by_side,
-            grid=(2,),
-            out_shape=jax.ShapeDtypeStruct((local * bs, group_width), bf16),
-            in_specs=[pl.BlockSpec((halves, local // 2, bs, width), lambda i: (0, i, 0, 0))],
-            out_specs=pl.BlockSpec((local // 2 * bs, group_width), lambda i: (i, 0)),
-            compiler_params=pltpu.CompilerParams(vmem_limit_bytes=8 * 2**20),
-        )(out)
+        return out.reshape(local * bs, group_width)
 
     return jax.shard_map(
         per_device,

time: 49.4 us -> 46.9 us (0.949)
  Pallas kernels: 48.1 us -> 44.8 us
  local copies, waits for them, and re-layouts: 1.03 us -> 1.87 us
    pallas_call x2 -> x1, Pallas kernels: 48.1 us -> 44.8 us  [per_device(): pl.pallas_call(functools.partial(filter_kernel, rows, groups, halves), ou...]
    unnamed x2 -> x1, local copies, waits for them, and re-layouts: 1.03 us -> 1.87 us
where the time goes in v6:
time: 46.9 us; the launch traced here: 46.7 us
  Pallas kernels  44.8 us (96%)
  local copies, waits for them, and re-layouts  1.87 us (4%)
    pallas_call x1, Pallas kernels, per_device(): pl.pallas_call(functools.partial(filter_kernel, rows, groups, halves), ou...  44.8 us
    unnamed x1, local copies, waits for them, and re-layouts  1.87 us

profile of v6, /device:TPU:25, one launch (start us, length us, event | category | flops | bytes accessed | tf_op | source)
XLA Modules:
  0.0 46.7 jit_solution(15636394790929189815)
XLA Ops:
  0.0 44.8 %shard_map.46 = bf16[8,128,256]{2,1,0:T(8,128)(2,1)} custom-call(bf16[256,1024]{1,0:T(8,128)(2,1)} %vec_hbm.1, bf16[1024,1024]{1,0:T(8,128)(2,1)} %rot_hbm.1, bf16[8,8,128,128]{3,2,1,0:T(8,128)(2,1)} %blk_hbm.1, s32[8,8]{1,0:T(8,128)} %cols_in.1), custom_call_target="tpu_custom_call" | custom-call | flops 2684354560 | bytes 8388608 | tf_op jit(solution)/shard_map/pallas_call | solution.py:358
  44.8 1.9 %copy.6 = bf16[1024,256]{1,0:T(8,128)(2,1)} copy(bf16[1024,256]{1,0:T(8,128)(2,1)} %bitcast.1) | data formatting | bytes 1048576

commit v7 on v6

--- a/solution.py
+++ b/solution.py
@@ -339,6 +339,14 @@
         for h in range(halves):
             for k in range(pairs):
                 out_local(h, k).wait()
+
+
+def hand_over(src, dst, sems):
+    copies = [pltpu.make_async_copy(src.at[i], dst.at[i], sems.at[i]) for i in range(src.shape[0])]
+    for copy in copies:
+        copy.start()
+    for copy in copies:
+        copy.wait()
 
 
 def solution(mesh):
@@ -390,6 +398,14 @@
             cost_estimate=pl.CostEstimate(
                 flops=flops, bytes_accessed=8 * 2**20, transcendentals=0),
         )(vectors, rotation, blocks, columns)
+        out = pl.pallas_call(
+            hand_over,
+            out_shape=jax.ShapeDtypeStruct(out.shape, bf16),
+            in_specs=[pl.BlockSpec(memory_space=pl.ANY)],
+            out_specs=pl.BlockSpec(memory_space=pl.ANY),
+            scratch_shapes=[dma((local,))],
+            compiler_params=pltpu.CompilerParams(vmem_limit_bytes=127 * 2**19),
+        )(out)
         return out.reshape(local * bs, group_width)
 
     return jax.shard_map(

time: 46.9 us -> 62 us (1.32)
  Pallas kernels: 44.8 us -> 61.9 us
  local copies, waits for them, and re-layouts: 1.87 us -> 0 us
    pallas_call x0 -> x1, Pallas kernels: none -> 17.1 us  [per_device(): pl.pallas_call(hand_over, out_shape=jax.ShapeDtypeStruct(out.shape, bf16)...]
    unnamed x1 -> x0, local copies, waits for them, and re-layouts: 1.87 us -> none
where the time goes in v7:
time: 62 us; the launch traced here: 61.9 us
  Pallas kernels  61.9 us (100%)
    pallas_call x1, Pallas kernels, per_device(): pl.pallas_call(functools.partial(filter_kernel, rows, groups, halves), ou...  44.8 us
    pallas_call x1, Pallas kernels, per_device(): pl.pallas_call(hand_over, out_shape=jax.ShapeDtypeStruct(out.shape, bf16)...  17.1 us

profile of v7, /device:TPU:25, one launch (start us, length us, event | category | flops | bytes accessed | tf_op | source)
XLA Modules:
  0.0 61.9 jit_solution(17599907067215695558)
XLA Ops:
  0.0 44.8 %shard_map.46.src = bf16[8,128,256]{2,1,0:T(8,128)(2,1)} custom-call(bf16[256,1024]{1,0:T(8,128)(2,1)} %vec_hbm.1, bf16[1024,1024]{1,0:T(8,128)(2,1)} %rot_hbm.1, bf16[8,8,128,128]{3,2,1,0:T(8,128)(2,1)} %blk_hbm.1, s32[8,8]{1,0:T(8,128)} %cols_in.1), custom_call_target="tpu_custom_call" | custom-call | flops 2684354560 | bytes 8388608 | tf_op jit(solution)/shard_map/pallas_call | solution.py:366
  44.8 17.1 %shard_map.47 = bf16[8,128,256]{2,1,0:T(8,128)(2,1)} custom-call(bf16[8,128,256]{2,1,0:T(8,128)(2,1)} %shard_map.46.src), custom_call_target="tpu_custom_call" | custom-call | tf_op jit(solution)/shard_map/pallas_call | solution.py:401
